TPU v7x, 32 devices: a whole 2x2x4 slice. The times are simulated.
32 devices in a mesh: ctx: 8 (over z, x), tp: 4 (over y, core).
Axes of the slice: x: 2, y: 2, z: 4, core: 2. Of those that a mesh axis runs over, the one named last changes fastest.
Arguments:
- query_rows: bfloat16 [2048, 4096], P('ctx', 'tp'), may hold values from -6 to 6
- key_rows: bfloat16 [2048, 4096], P('ctx', 'tp'), may hold values from -6 to 6
- value_rows: bfloat16 [2048, 4096], P('ctx', 'tp'), may hold values from -6 to 6
- filters: bfloat16 [2048, 4096], P('ctx', 'tp'), may hold values from -1 to 1
- skip_gain: float32 [4096], P('tp'), may hold values from 0.5 to 1.5
- out_weight: bfloat16 [4096, 4096], P('tp', 'ctx'), may hold values from -0.125 to 0.125
Outputs:
- mixed_out: bfloat16 [2048, 4096], P('ctx', 'tp')
All inputs are finite; a program needn't handle non-finite values.
Results may differ from a plain program's by a relative error of at most 0.0057.
Values may be sent and summed in bfloat16 or wider, within the bound.
A program may use at most 128 MiB of HBM per device.

v0:
```python
import functools
import math

import jax
import jax.numpy as jnp
import ml_dtypes
import numpy as np
from jax import lax
from jax.experimental import pallas as pl
from jax.experimental.pallas import tpu as pltpu
from jax.sharding import PartitionSpec as P

precise = lax.Precision.HIGHEST
MESH = pl.DeviceIdType.MESH
LANES = 128
INNER = 8
f32 = jnp.float32
bf16 = jnp.bfloat16


def make_tables(full_len, size_one, second):
    index_one = jnp.arange(size_one, dtype=jnp.int32)
    half_one = jnp.arange(size_one // 2, dtype=jnp.int32)
    index_two = jnp.arange(second, dtype=jnp.int32)
    angle_one = (
        2.0
        * math.pi
        / size_one
        * (index_one[:, None] * half_one[None, :] % size_one).astype(jnp.float32)
    )
    angle_two = (
        2.0
        * math.pi
        / second
        * (index_two[:, None] * index_two[None, :] % second).astype(jnp.float32)
    )
    angle_mid = (
        2.0
        * math.pi
        / full_len
        * (index_one[:, None] * index_two[None, :] % full_len).astype(jnp.float32)
    )
    return (
        jnp.cos(angle_one),
        jnp.sin(angle_one),
        jnp.cos(angle_two),
        jnp.sin(angle_two),
        jnp.cos(angle_mid),
        jnp.sin(angle_mid),
    )


def along_second(matrix, table):
    return jnp.einsum("mkb,bj->mkj", matrix, table, precision=precise)


def forward_spectrum(signal, tables, size_one, second):
    cos_one, sin_one, cos_two, sin_two, cos_mid, sin_mid = tables
    reshaped = signal.reshape(signal.shape[0], size_one // 2, second)
    real_a = jnp.einsum("ka,mab->mkb", cos_one, reshaped, precision=precise)
    imag_a = -jnp.einsum("ka,mab->mkb", sin_one, reshaped, precision=precise)
    real_b = real_a * cos_mid + imag_a * sin_mid
    imag_b = imag_a * cos_mid - real_a * sin_mid
    real_c = along_second(real_b, cos_two) + along_second(imag_b, sin_two)
    imag_c = along_second(imag_b, cos_two) - along_second(real_b, sin_two)
    return (real_c, imag_c)


def inverse_signal(real_p, imag_p, tables, full_len):
    cos_one, sin_one, cos_two, sin_two, cos_mid, sin_mid = tables
    real_q = along_second(real_p, cos_two) - along_second(imag_p, sin_two)
    imag_q = along_second(imag_p, cos_two) + along_second(real_p, sin_two)
    real_r = real_q * cos_mid - imag_q * sin_mid
    imag_r = real_q * sin_mid + imag_q * cos_mid
    result = jnp.einsum("ka,mkb->mab", cos_one, real_r, precision=precise) - jnp.einsum(
        "ka,mkb->mab", sin_one, imag_r, precision=precise
    )
    return (result / full_len).reshape(real_p.shape[0], full_len // 2)


def convolve_block(series, taps):
    length = series.shape[-1]
    full_len = 2 * length
    size_one = 1 << (full_len.bit_length() - 1) // 2
    second = full_len // size_one
    tables = make_tables(full_len, size_one, second)
    channels = series.shape[0]
    stacked = jnp.concatenate([series.astype(jnp.float32), taps.astype(jnp.float32)], axis=0)
    real_s, imag_s = forward_spectrum(stacked, tables, size_one, second)
    real_u, real_h = (real_s[:channels], real_s[channels:])
    imag_u, imag_h = (imag_s[:channels], imag_s[channels:])
    real_p = real_u * real_h - imag_u * imag_h
    imag_p = real_u * imag_h + imag_u * real_h
    return inverse_signal(real_p, imag_p, tables, full_len)


def plain_path(query_rows, key_rows, value_rows, filters, skip_gain, out_weight):
    row_count, chan_count = key_rows.shape
    groups = lax.axis_size("ctx")
    per_group = chan_count // groups
    mixed_in = (key_rows.astype(jnp.float32) * value_rows.astype(jnp.float32)).astype(jnp.bfloat16)
    series_t = mixed_in.T.reshape(groups, per_group, row_count)
    taps_t = filters.T.reshape(groups, per_group, row_count)
    series_p = lax.all_to_all(series_t, "ctx", split_axis=0, concat_axis=2, tiled=True)
    taps_p = lax.all_to_all(taps_t, "ctx", split_axis=0, concat_axis=2, tiled=True)
    result = convolve_block(series_p[0], taps_p[0])[None]
    returned = lax.all_to_all(result, "ctx", split_axis=2, concat_axis=0, tiled=True)
    convolved = returned.reshape(chan_count, row_count).T
    gated_rows = (
        query_rows.astype(jnp.float32)
        * (convolved + skip_gain[None, :] * mixed_in.astype(jnp.float32))
    ).astype(jnp.bfloat16)
    partial_value = jnp.dot(
        gated_rows,
        lax.all_gather(out_weight, "ctx", axis=1, tiled=True),
        preferred_element_type=jnp.float32,
    )
    return lax.psum_scatter(partial_value, "tp", scatter_dimension=1, tiled=True).astype(
        jnp.bfloat16
    )


def split_table(table):
    high = table.astype(ml_dtypes.bfloat16)
    low = (table - high.astype(np.float64)).astype(ml_dtypes.bfloat16)
    return high, low


def block_tables(blocks):
    angle = np.pi * (np.arange(blocks) + 0.5) / blocks
    phase = np.outer(angle, np.arange(blocks))
    forward = np.concatenate([np.cos(phase), -np.sin(phase)], axis=0)
    inverse = np.concatenate([np.cos(phase.T), -np.sin(phase.T)], axis=1) / blocks
    forward_high, forward_low = split_table(forward)
    inverse_high, inverse_low = split_table(inverse)
    twist = np.stack([np.cos(angle), -np.sin(angle)])[:, :, None]
    twist = np.broadcast_to(twist, (2, blocks, LANES)).astype(np.float32)
    return (
        np.concatenate([forward_high, forward_low], axis=1),
        np.concatenate([inverse_high, inverse_high, inverse_low], axis=1),
        np.ascontiguousarray(twist),
    )


def convolve_kernel(
    groups, send_ref, weight_ref, skip_ref, forward_ref, inverse_ref, twist_ref,
    gated_ref, other_ref,
    series, taps, gates, spec_u, spec_h,
    send_sem, recv_sem, pair_sem,
):
    me = lax.axis_index("ctx")
    partner = me + 1 - 2 * lax.rem(me, 2)
    part = send_ref.shape[2]
    blocks = groups * part
    landing = (series, taps, gates)

    barrier = pltpu.get_barrier_semaphore()
    for step in range(1, groups):
        peer = lax.rem(me + step, groups)
        pl.semaphore_signal(barrier, inc=1, device_id={"ctx": peer}, device_id_type=MESH)
    pl.semaphore_wait(barrier, groups - 1)

    def copy_to(which, step):
        peer = lax.rem(me + step, groups)
        return pltpu.make_async_remote_copy(
            src_ref=send_ref.at[which, peer],
            dst_ref=landing[which].at[me],
            send_sem=send_sem.at[which, step],
            recv_sem=recv_sem.at[which, me],
            device_id={"ctx": peer},
            device_id_type=MESH,
        )

    def wait_from(which, step):
        source = lax.rem(me + step, groups)
        pltpu.make_async_remote_copy(
            src_ref=send_ref.at[which, source],
            dst_ref=landing[which].at[source],
            send_sem=send_sem.at[which, step],
            recv_sem=recv_sem.at[which, source],
            device_id={"ctx": source},
            device_id_type=MESH,
        ).wait_recv()

    for which in (0, 1):
        for step in range(1, groups):
            copy_to(which, step).start()
    pair = pltpu.make_async_remote_copy(
        src_ref=weight_ref,
        dst_ref=other_ref,
        send_sem=pair_sem.at[0],
        recv_sem=pair_sem.at[1],
        device_id={"ctx": partner},
        device_id_type=MESH,
    )
    pair.start()
    for step in range(1, groups):
        copy_to(2, step).start()
    for which in range(3):
        landing[which][me] = send_ref[which, me]

    def transform(which, spectrum):
        for step in range(1, groups):
            wait_from(which, step)

        @pl.loop(0, INNER // 2)
        def _(tile):
            columns = pl.ds(pl.multiple_of(tile * 2 * LANES, 2 * LANES), 2 * LANES)
            rows = landing[which][:, :, columns].reshape(blocks, 2 * LANES)
            spectrum[:, columns] = jnp.dot(
                forward_ref[...],
                jnp.concatenate([rows, rows], axis=0),
                preferred_element_type=f32,
            )

    transform(0, spec_u)
    transform(1, spec_h)

    @pl.loop(0, blocks // 8)
    def _(tile):
        real = pl.ds(pl.multiple_of(tile * 8, 8), 8)
        imag = pl.ds(pl.multiple_of(blocks + tile * 8, 8), 8)
        lanes = [slice(b * LANES, (b + 1) * LANES) for b in range(INNER)]
        ur = [spec_u[real, lane] for lane in lanes]
        ui = [spec_u[imag, lane] for lane in lanes]
        hr = [spec_h[real, lane] for lane in lanes]
        hi = [spec_h[imag, lane] for lane in lanes]
        cos, sin = twist_ref[0, real], twist_ref[1, real]

        def term(degree):
            pairs = [(b, degree - b) for b in range(INNER) if 0 <= degree - b < INNER]
            re = sum(ur[b] * hr[d] - ui[b] * hi[d] for b, d in pairs)
            im = sum(ur[b] * hi[d] + ui[b] * hr[d] for b, d in pairs)
            return re, im

        for b in range(INNER):
            re, im = term(b)
            if b + INNER <= 2 * INNER - 2:
                up_re, up_im = term(b + INNER)
                re = re + up_re * cos - up_im * sin
                im = im + up_re * sin + up_im * cos
            spec_u[real, lanes[b]] = re
            spec_u[imag, lanes[b]] = im

    for step in range(1, groups):
        wait_from(2, step)

    @pl.loop(0, INNER // 2)
    def _(tile):
        columns = pl.ds(pl.multiple_of(tile * 2 * LANES, 2 * LANES), 2 * LANES)
        spectrum = spec_u[:, columns]
        high = spectrum.astype(bf16)
        low = (spectrum - high.astype(f32)).astype(bf16)
        convolved = jnp.dot(
            inverse_ref[...],
            jnp.concatenate([high, low, high], axis=0),
            preferred_element_type=f32,
        )
        mixed = series[:, :, columns].reshape(blocks, 2 * LANES).astype(f32)
        gate = gates[:, :, columns].reshape(blocks, 2 * LANES).astype(f32)
        gated_ref[:, columns] = (gate * (convolved + skip_ref[:, columns] * mixed)).astype(bf16)

    for which in range(3):
        for step in range(1, groups):
            copy_to(which, step).wait_send()
    pair.wait()


def project_kernel(
    groups, gated_ref, own_ref, other_ref, out_ref,
    landed, operand, total, sending, chip_in, far_out, far_in, final,
    send_sem, recv_sem, chip_send, chip_recv, far_sem, last_sem, local_sem,
):
    me, mine = lax.axis_index("ctx"), lax.axis_index("tp")
    plane, side = me // 2, lax.rem(me, 2)
    chip, core = mine // 2, lax.rem(mine, 2)
    part = landed.shape[2]
    half = own_ref.shape[1]
    tokens = part * INNER
    sibling = chip * 2 + 1 - core
    across = (1 - chip) * 2 + core
    order = (
        2 * (1 - core) + 1 - chip,
        2 * (1 - core) + chip,
        2 * core + 1 - chip,
        2 * core + chip,
    )
    last_block = order[3]
    to_ctx, to_tp = last_block * 2 + side, plane
    from_ctx, from_tp = mine * 2 + side, 2 * lax.rem(plane, 2) + plane // 2
    stays = jnp.logical_and(to_ctx == me, to_tp == mine)
    leaves = jnp.logical_not(stays)

    barrier = pltpu.get_barrier_semaphore()
    for step in range(1, groups):
        peer = lax.rem(me + step, groups)
        pl.semaphore_signal(barrier, inc=1, device_id={"ctx": peer}, device_id_type=MESH)
    for peer in (sibling, across):
        pl.semaphore_signal(barrier, inc=1, device_id={"tp": peer}, device_id_type=MESH)

    @pl.when(leaves)
    def _():
        pl.semaphore_signal(
            barrier, inc=1, device_id={"ctx": from_ctx, "tp": from_tp}, device_id_type=MESH
        )

    pl.semaphore_wait(barrier, groups + 1 + leaves.astype(jnp.int32))

    def rows_of(index, towards):
        return pl.ds(pl.multiple_of((order[index] * 2 + lax.rem(towards, 2)) * part, part), part)

    def copy_to(index, step):
        peer = lax.rem(me + step, groups)
        return pltpu.make_async_remote_copy(
            src_ref=gated_ref.at[rows_of(index, peer)],
            dst_ref=landed.at[index, me],
            send_sem=send_sem.at[index, step],
            recv_sem=recv_sem.at[index, me],
            device_id={"ctx": peer},
            device_id_type=MESH,
        )

    for index in range(4):
        for step in range(1, groups):
            copy_to(index, step).start()
    for index in range(4):
        landed[index, me] = gated_ref[rows_of(index, me)]

    def partial(index):
        for step in range(1, groups):
            source = lax.rem(me + step, groups)
            pltpu.make_async_remote_copy(
                src_ref=landed.at[index, source],
                dst_ref=landed.at[index, source],
                send_sem=send_sem.at[index, step],
                recv_sem=recv_sem.at[index, source],
                device_id={"ctx": source},
                device_id_type=MESH,
            ).wait_recv()
        for source in range(groups):
            for b in range(INNER):
                operand[b * part : (b + 1) * part, source * LANES : (source + 1) * LANES] = landed[
                    index, source, :, b * LANES : (b + 1) * LANES
                ]
        for weight, which in ((own_ref, side), (other_ref, 1 - side)):
            columns = pl.ds(pl.multiple_of(which * half, half), half)
            total[:, columns] = jnp.dot(operand[...], weight[...], preferred_element_type=f32)

    def to_sibling(index):
        return pltpu.make_async_remote_copy(
            src_ref=sending.at[index],
            dst_ref=chip_in.at[index],
            send_sem=chip_send.at[index],
            recv_sem=chip_recv.at[index],
            device_id={"tp": sibling},
            device_id_type=MESH,
        )

    for index in range(2):
        partial(index)
        sending[index] = total[...].astype(bf16)
        to_sibling(index).start()

    partial(2)
    to_sibling(0).wait_recv()
    far_out[...] = (total[...] + chip_in[0].astype(f32)).astype(bf16)
    far = pltpu.make_async_remote_copy(
        src_ref=far_out,
        dst_ref=far_in,
        send_sem=far_sem.at[0],
        recv_sem=far_sem.at[1],
        device_id={"tp": across},
        device_id_type=MESH,
    )
    far.start()

    partial(3)
    to_sibling(1).wait_recv()
    far.wait_recv()
    final[...] = (total[...] + chip_in[1].astype(f32) + far_in[...].astype(f32)).astype(bf16)

    @pl.when(leaves)
    def _():
        last = pltpu.make_async_remote_copy(
            src_ref=final,
            dst_ref=out_ref,
            send_sem=last_sem.at[0],
            recv_sem=last_sem.at[1],
            device_id={"ctx": to_ctx, "tp": to_tp},
            device_id_type=MESH,
        )
        last.start()
        last.wait()

    @pl.when(stays)
    def _():
        keep = pltpu.make_async_copy(final, out_ref, local_sem)
        keep.start()
        keep.wait()

    for index in range(4):
        for step in range(1, groups):
            copy_to(index, step).wait_send()
    for index in range(2):
        to_sibling(index).wait_send()
    far.wait_send()


def kernel_path(query_rows, key_rows, value_rows, filters, skip_gain, out_weight):
    row_count, chan_count = key_rows.shape
    groups = lax.axis_size("ctx")
    me = lax.axis_index("ctx")
    part = row_count // INNER
    wide = INNER * LANES
    blocks = groups * part
    half = out_weight.shape[1]
    mixed_in = (key_rows.astype(f32) * value_rows.astype(f32)).astype(bf16)

    def by_group(rows):
        cut = rows.reshape(part, INNER, groups, LANES)
        return cut.transpose(2, 0, 1, 3).reshape(groups, part, wide)

    sent = jnp.stack([by_group(mixed_in), by_group(filters), by_group(query_rows)])
    skip = jnp.tile(lax.dynamic_slice(skip_gain, (me * LANES,), (LANES,)), INNER)[None, :]
    forward, inverse, twist = block_tables(blocks)
    vmem = pl.BlockSpec(memory_space=pltpu.VMEM)
    hbm = pl.BlockSpec(memory_space=pl.ANY)
    dma = pltpu.SemaphoreType.DMA
    gated, other = pl.pallas_call(
        functools.partial(convolve_kernel, groups),
        out_shape=(
            jax.ShapeDtypeStruct((blocks, wide), bf16),
            jax.ShapeDtypeStruct(out_weight.shape, bf16),
        ),
        in_specs=[vmem, hbm, vmem, vmem, vmem, vmem],
        out_specs=(vmem, hbm),
        scratch_shapes=[
            pltpu.VMEM((groups, part, wide), bf16),
            pltpu.VMEM((groups, part, wide), bf16),
            pltpu.VMEM((groups, part, wide), bf16),
            pltpu.VMEM((2 * blocks, wide), f32),
            pltpu.VMEM((2 * blocks, wide), f32),
            dma((3, groups)),
            dma((3, groups)),
            dma((2,)),
        ],
        compiler_params=pltpu.CompilerParams(
            collective_id=0, has_side_effects=True, vmem_limit_bytes=40 * 2**20
        ),
        name="convolve",
    )(sent, out_weight, skip, jnp.asarray(forward), jnp.asarray(inverse), jnp.asarray(twist))
    result = pl.pallas_call(
        functools.partial(project_kernel, groups),
        out_shape=jax.ShapeDtypeStruct((row_count, 2 * half), bf16),
        in_specs=[vmem, vmem, vmem],
        out_specs=hbm,
        scratch_shapes=[
            pltpu.VMEM((4, groups, part, wide), bf16),
            pltpu.VMEM((row_count, chan_count), bf16),
            pltpu.VMEM((row_count, 2 * half), f32),
            pltpu.VMEM((2, row_count, 2 * half), bf16),
            pltpu.VMEM((2, row_count, 2 * half), bf16),
            pltpu.VMEM((row_count, 2 * half), bf16),
            pltpu.VMEM((row_count, 2 * half), bf16),
            pltpu.VMEM((row_count, 2 * half), bf16),
            dma((4, groups)),
            dma((4, groups)),
            dma((2,)),
            dma((2,)),
            dma((2,)),
            dma((2,)),
            dma,
        ],
        compiler_params=pltpu.CompilerParams(
            collective_id=1, has_side_effects=True, vmem_limit_bytes=40 * 2**20
        ),
        name="project",
    )(gated, out_weight, other)
    return result.reshape(INNER, part, 2 * half).transpose(1, 0, 2).reshape(row_count, 2 * half)


def on_device(query_rows, key_rows, value_rows, filters, skip_gain, out_weight):
    row_count, chan_count = key_rows.shape
    groups, shares = lax.axis_size("ctx"), lax.axis_size("tp")
    fits = (
        shares == 4
        and groups == 2 * shares
        and chan_count == groups * LANES
        and row_count % (16 * INNER) == 0
        and groups * row_count <= 2048
    )
    path = kernel_path if fits else plain_path
    return path(query_rows, key_rows, value_rows, filters, skip_gain, out_weight)


def solution(mesh):
    in_specs = (
        P("ctx", "tp"),
        P("ctx", "tp"),
        P("ctx", "tp"),
        P("ctx", "tp"),
        P("tp"),
        P("tp", "ctx"),
    )
    out_specs = P("ctx", "tp")
    return jax.shard_map(
        on_device, mesh=mesh, in_specs=in_specs, out_specs=out_specs, check_vma=False
    )
```

profile of v0, /device:TPU:7, one launch (start us, length us, event | category | flops | bytes accessed | tf_op | source)
XLA Modules:
  0.0 128.7 jit_solution(13206649550516326913)
XLA Ops:
  0.0 0.0 copy-start
  0.0 0.0 copy-start.5
  0.0 0.0 copy-start.6
  0.0 0.9 dynamic_slice.3
  0.9 0.2 copy-done
  1.1 0.1 copy_bitcast_fusion.1
  1.2 0.0 copy-start.7
  1.2 0.2 stack_reshape.11
  1.4 0.0 copy-done.5
  1.4 0.0 copy-done.6
  1.4 0.1 copy_bitcast_fusion.3
  1.6 0.2 stack_reshape.9
  1.8 0.5 copy-done.7
  2.3 0.1 copy_bitcast_fusion.2
  2.4 0.2 stack_reshape.10
  2.6 0.0 copy-start.1
  2.6 0.0 copy-start.2
  2.6 0.0 copy-start.3
  2.6 0.0 copy-start.4
  2.6 0.2 pad_maximum_fusion.send_ref
  2.8 1.0 copy-done.1
  3.8 0.2 copy-done.2
  4.0 0.1 copy-done.3
  4.2 0.1 copy-done.4
  4.2 46.2 %convolve.1 = (bf16[256,1024]{1,0:T(8,128)(2,1)S(1)}, bf16[1024,512]{1,0:T(8,128)(2,1)S(1)}) custom-call(bf16[3,8,32,1024]{3,2,1,0:T(8,128)(2,1)S(1)} %pad_maximum_fusion.send_ref, bf16[1024,512]{1,0:T(8,128)(2,1)S(1)} %copy-done.1, f32[1,1024]{1,0:T(1,128)S(1)} %bitcast.29, bf16[512,512]{1,0:T(8,128)(2,1)S(1)} %copy-done.3, ...), custom_call_target="tpu_custom_call" | custom-call | tf_op jit(solution)/shard_map/convolve/pallas_call | solution.py:429
  50.4 77.2 %project.1 = bf16[256,1024]{1,0:T(8,128)(2,1)S(1)} custom-call(bf16[256,1024]{1,0:T(8,128)(2,1)S(1)} %get-tuple-element.7.gated_ref, bf16[1024,512]{1,0:T(8,128)(2,1)S(1)} %copy-done.1, bf16[1024,512]{1,0:T(8,128)(2,1)S(1)} %get-tuple-element.8.other_ref), custom_call_target="tpu_custom_call" | custom-call | tf_op jit(solution)/shard_map/project/pallas_call | solution.py:452
  127.6 1.1 copy.18
  (1 shorter events, 0.0 us)
Async XLA Ops:
  0.0 1.1 copy-start
  0.0 1.4 %copy-start.5 = (bf16[256,1024]{1,0:T(8,128)(2,1)S(1)}, bf16[256,1024]{1,0:T(8,128)(2,1)}, u32[]{:S(2)}) copy-start(bf16[256,1024]{1,0:T(8,128)(2,1)} %param.11) | copy-start | bytes 1572868
  0.0 1.4 %copy-start.6 = (bf16[256,1024]{1,0:T(8,128)(2,1)S(1)}, bf16[256,1024]{1,0:T(8,128)(2,1)}, u32[]{:S(2)}) copy-start(bf16[256,1024]{1,0:T(8,128)(2,1)} %param.10) | copy-start | bytes 1572868
  1.2 1.1 copy-start.7
  2.6 1.2 copy-start.1
  2.6 1.4 %copy-start.2 = (bf16[256,1536]{1,0:T(8,128)(2,1)S(1)}, bf16[256,1536]{1,0:T(8,128)(2,1)}, u32[]{:S(2)}) copy-start(bf16[256,1536]{1,0:T(8,128)(2,1)} %constant.19.clone.inverse_ref) | copy-start | bytes 2359300
  2.6 1.6 %copy-start.3 = (bf16[512,512]{1,0:T(8,128)(2,1)S(1)}, bf16[512,512]{1,0:T(8,128)(2,1)}, u32[]{:S(2)}) copy-start(bf16[512,512]{1,0:T(8,128)(2,1)} %constant.18.clone.forward_ref) | copy-start | bytes 1572868
  2.6 1.6 %copy-start.4 = (f32[2,256,128]{2,1,0:T(8,128)S(1)}, f32[2,256,128]{2,1,0:T(8,128)}, u32[]{:S(2)}) copy-start(f32[2,256,128]{2,1,0:T(8,128)} %constant.20.clone.twist_ref) | copy-start | bytes 786436
where the time goes:
time: 129 us
  Pallas kernels  123 us (95%)
  local copies, waits for them, and re-layouts  4.9 us (4%)
    pallas_call x1, Pallas kernels, kernel_path(): pl.pallas_call(functools.partial(project_kernel, groups), out_shape=jax.S...  77.2 us
    pallas_call x1, Pallas kernels, kernel_path(): pl.pallas_call(functools.partial(convolve_kernel, groups), out_shape=(jax...  46.2 us

commit v1 on v0

--- a/solution.py
+++ b/solution.py
@@ -142,23 +142,52 @@
     )
 
 
-def convolve_kernel(
-    groups, send_ref, weight_ref, skip_ref, forward_ref, inverse_ref, twist_ref,
-    gated_ref, other_ref,
-    series, taps, gates, spec_u, spec_h,
-    send_sem, recv_sem, pair_sem,
+def mixer_kernel(
+    groups, send_ref, own_ref, skip_ref, forward_ref, inverse_ref, twist_ref, out_ref,
+    series, taps, gates, spec_u, spec_h, gated_ref, other_ref,
+    landed, operand, total, sending, chip_in, far_out, far_in, final,
+    send_sem, recv_sem, pair_send, pair_recv, piece_send, piece_recv, pass_send,
+    chip_send, chip_recv, far_send, far_recv, last_send, last_recv, local_sem,
 ):
-    me = lax.axis_index("ctx")
-    partner = me + 1 - 2 * lax.rem(me, 2)
+    me, mine = lax.axis_index("ctx"), lax.axis_index("tp")
+    plane, side = me // 2, lax.rem(me, 2)
+    chip, core = mine // 2, lax.rem(mine, 2)
+    partner = plane * 2 + 1 - side
+    near = plane + 1 - 2 * lax.rem(plane, 2)
+    beyond = lax.rem(plane + 2, groups // 2)
+    mate = near * 2 + side
     part = send_ref.shape[2]
     blocks = groups * part
+    depth, half = own_ref.shape
+    splits, small = landed.shape[0], landed.shape[3]
     landing = (series, taps, gates)
+    sibling = chip * 2 + 1 - core
+    opposite = (1 - chip) * 2 + core
+    order = (
+        2 * (1 - core) + 1 - chip,
+        2 * (1 - core) + chip,
+        2 * core + 1 - chip,
+        2 * core + chip,
+    )
+    to_ctx, to_tp = order[3] * 2 + side, plane
+    from_ctx, from_tp = mine * 2 + side, 2 * lax.rem(plane, 2) + plane // 2
+    stays = jnp.logical_and(to_ctx == me, to_tp == mine)
+    leaves = jnp.logical_not(stays)
 
     barrier = pltpu.get_barrier_semaphore()
     for step in range(1, groups):
         peer = lax.rem(me + step, groups)
         pl.semaphore_signal(barrier, inc=1, device_id={"ctx": peer}, device_id_type=MESH)
-    pl.semaphore_wait(barrier, groups - 1)
+    for peer in (sibling, opposite):
+        pl.semaphore_signal(barrier, inc=1, device_id={"tp": peer}, device_id_type=MESH)
+
+    @pl.when(leaves)
+    def _():
+        pl.semaphore_signal(
+            barrier, inc=1, device_id={"ctx": from_ctx, "tp": from_tp}, device_id_type=MESH
+        )
+
+    pl.semaphore_wait(barrier, groups + 1 + leaves.astype(jnp.int32))
 
     def copy_to(which, step):
         peer = lax.rem(me + step, groups)
@@ -182,27 +211,25 @@
             device_id_type=MESH,
         ).wait_recv()
 
+    def weight_copy(which):
+        rows = pl.ds(which * (depth // 2), depth // 2)
+        return pltpu.make_async_remote_copy(
+            src_ref=own_ref.at[rows],
+            dst_ref=other_ref.at[rows],
+            send_sem=pair_send.at[which],
+            recv_sem=pair_recv.at[which],
+            device_id={"ctx": partner},
+            device_id_type=MESH,
+        )
+
     for which in (0, 1):
         for step in range(1, groups):
             copy_to(which, step).start()
-    pair = pltpu.make_async_remote_copy(
-        src_ref=weight_ref,
-        dst_ref=other_ref,
-        send_sem=pair_sem.at[0],
-        recv_sem=pair_sem.at[1],
-        device_id={"ctx": partner},
-        device_id_type=MESH,
-    )
-    pair.start()
-    for step in range(1, groups):
-        copy_to(2, step).start()
+    weight_copy(0).start()
     for which in range(3):
         landing[which][me] = send_ref[which, me]
 
     def transform(which, spectrum):
-        for step in range(1, groups):
-            wait_from(which, step)
-
         @pl.loop(0, INNER // 2)
         def _(tile):
             columns = pl.ds(pl.multiple_of(tile * 2 * LANES, 2 * LANES), 2 * LANES)
@@ -213,7 +240,15 @@
                 preferred_element_type=f32,
             )
 
+    for step in range(1, groups):
+        wait_from(0, step)
     transform(0, spec_u)
+    for step in range(1, groups):
+        wait_from(1, step)
+        if step == groups // 2:
+            for later in range(1, groups):
+                copy_to(2, later).start()
+    weight_copy(1).start()
     transform(1, spec_h)
 
     @pl.loop(0, blocks // 8)
@@ -260,150 +295,155 @@
         gate = gates[:, :, columns].reshape(blocks, 2 * LANES).astype(f32)
         gated_ref[:, columns] = (gate * (convolved + skip_ref[:, columns] * mixed)).astype(bf16)
 
-    for which in range(3):
-        for step in range(1, groups):
-            copy_to(which, step).wait_send()
-    pair.wait()
-
-
-def project_kernel(
-    groups, gated_ref, own_ref, other_ref, out_ref,
-    landed, operand, total, sending, chip_in, far_out, far_in, final,
-    send_sem, recv_sem, chip_send, chip_recv, far_sem, last_sem, local_sem,
-):
-    me, mine = lax.axis_index("ctx"), lax.axis_index("tp")
-    plane, side = me // 2, lax.rem(me, 2)
-    chip, core = mine // 2, lax.rem(mine, 2)
-    part = landed.shape[2]
-    half = own_ref.shape[1]
-    tokens = part * INNER
-    sibling = chip * 2 + 1 - core
-    across = (1 - chip) * 2 + core
-    order = (
-        2 * (1 - core) + 1 - chip,
-        2 * (1 - core) + chip,
-        2 * core + 1 - chip,
-        2 * core + chip,
-    )
-    last_block = order[3]
-    to_ctx, to_tp = last_block * 2 + side, plane
-    from_ctx, from_tp = mine * 2 + side, 2 * lax.rem(plane, 2) + plane // 2
-    stays = jnp.logical_and(to_ctx == me, to_tp == mine)
-    leaves = jnp.logical_not(stays)
-
-    barrier = pltpu.get_barrier_semaphore()
-    for step in range(1, groups):
-        peer = lax.rem(me + step, groups)
-        pl.semaphore_signal(barrier, inc=1, device_id={"ctx": peer}, device_id_type=MESH)
-    for peer in (sibling, across):
-        pl.semaphore_signal(barrier, inc=1, device_id={"tp": peer}, device_id_type=MESH)
-
-    @pl.when(leaves)
-    def _():
-        pl.semaphore_signal(
-            barrier, inc=1, device_id={"ctx": from_ctx, "tp": from_tp}, device_id_type=MESH
-        )
-
-    pl.semaphore_wait(barrier, groups + 1 + leaves.astype(jnp.int32))
-
-    def rows_of(index, towards):
-        return pl.ds(pl.multiple_of((order[index] * 2 + lax.rem(towards, 2)) * part, part), part)
-
-    def copy_to(index, step):
-        peer = lax.rem(me + step, groups)
-        return pltpu.make_async_remote_copy(
-            src_ref=gated_ref.at[rows_of(index, peer)],
-            dst_ref=landed.at[index, me],
-            send_sem=send_sem.at[index, step],
-            recv_sem=recv_sem.at[index, me],
-            device_id={"ctx": peer},
-            device_id_type=MESH,
-        )
-
-    for index in range(4):
-        for step in range(1, groups):
-            copy_to(index, step).start()
-    for index in range(4):
-        landed[index, me] = gated_ref[rows_of(index, me)]
-
-    def partial(index):
-        for step in range(1, groups):
-            source = lax.rem(me + step, groups)
-            pltpu.make_async_remote_copy(
-                src_ref=landed.at[index, source],
-                dst_ref=landed.at[index, source],
-                send_sem=send_sem.at[index, step],
-                recv_sem=recv_sem.at[index, source],
-                device_id={"ctx": source},
-                device_id_type=MESH,
-            ).wait_recv()
+    pieces = [(split, index) for split in range(splits) for index in range(4)]
+    direct = (
+        beyond * 2 + side, beyond * 2 + 1 - side,
+        near * 2 + side, near * 2 + 1 - side,
+        partner,
+    )
+
+    def rows_of(piece, towards):
+        split, index = piece
+        start = (order[index] * 2 + lax.rem(towards, 2)) * part + split * small
+        return pl.ds(pl.multiple_of(start, small), small)
+
+    def piece_to(piece, slot):
+        return pltpu.make_async_remote_copy(
+            src_ref=gated_ref.at[rows_of(piece, direct[slot])],
+            dst_ref=landed.at[piece[0], piece[1], me],
+            send_sem=piece_send.at[piece[0], piece[1], slot],
+            recv_sem=piece_recv.at[piece[0], piece[1], me],
+            device_id={"ctx": direct[slot]},
+            device_id_type=MESH,
+        )
+
+    def pass_on(piece, source, slot):
+        place = landed.at[piece[0], piece[1], source]
+        return pltpu.make_async_remote_copy(
+            src_ref=place,
+            dst_ref=place,
+            send_sem=pass_send.at[piece[0], piece[1], slot],
+            recv_sem=piece_recv.at[piece[0], piece[1], source],
+            device_id={"ctx": mate},
+            device_id_type=MESH,
+        )
+
+    def launch(piece):
+        for slot in range(5):
+            piece_to(piece, slot).start()
+        landed[piece[0], piece[1], me] = gated_ref[rows_of(piece, me)]
+
+    def forward(piece):
+        for slot in range(2):
+            copy = pass_on(piece, direct[slot], slot)
+            copy.wait_recv()
+            copy.start()
+
+    far_plane = lax.rem(near + 2, groups // 2)
+    passed = (far_plane * 2 + side, far_plane * 2 + 1 - side)
+
+    def partial(piece):
+        for source in direct[2:] + passed:
+            pass_on(piece, source, 0).wait_recv()
         for source in range(groups):
             for b in range(INNER):
-                operand[b * part : (b + 1) * part, source * LANES : (source + 1) * LANES] = landed[
-                    index, source, :, b * LANES : (b + 1) * LANES
+                operand[b * small : (b + 1) * small, source * LANES : (source + 1) * LANES] = landed[
+                    piece[0], piece[1], source, :, b * LANES : (b + 1) * LANES
                 ]
         for weight, which in ((own_ref, side), (other_ref, 1 - side)):
             columns = pl.ds(pl.multiple_of(which * half, half), half)
             total[:, columns] = jnp.dot(operand[...], weight[...], preferred_element_type=f32)
 
-    def to_sibling(index):
-        return pltpu.make_async_remote_copy(
-            src_ref=sending.at[index],
-            dst_ref=chip_in.at[index],
-            send_sem=chip_send.at[index],
-            recv_sem=chip_recv.at[index],
+    def to_sibling(split, index):
+        return pltpu.make_async_remote_copy(
+            src_ref=sending.at[split, index],
+            dst_ref=chip_in.at[split, index],
+            send_sem=chip_send.at[split, index],
+            recv_sem=chip_recv.at[split, index],
             device_id={"tp": sibling},
             device_id_type=MESH,
         )
 
-    for index in range(2):
-        partial(index)
-        sending[index] = total[...].astype(bf16)
-        to_sibling(index).start()
-
-    partial(2)
-    to_sibling(0).wait_recv()
-    far_out[...] = (total[...] + chip_in[0].astype(f32)).astype(bf16)
-    far = pltpu.make_async_remote_copy(
-        src_ref=far_out,
-        dst_ref=far_in,
-        send_sem=far_sem.at[0],
-        recv_sem=far_sem.at[1],
-        device_id={"tp": across},
-        device_id_type=MESH,
-    )
-    far.start()
-
-    partial(3)
-    to_sibling(1).wait_recv()
-    far.wait_recv()
-    final[...] = (total[...] + chip_in[1].astype(f32) + far_in[...].astype(f32)).astype(bf16)
-
-    @pl.when(leaves)
-    def _():
-        last = pltpu.make_async_remote_copy(
-            src_ref=final,
-            dst_ref=out_ref,
-            send_sem=last_sem.at[0],
-            recv_sem=last_sem.at[1],
+    def to_opposite(split):
+        return pltpu.make_async_remote_copy(
+            src_ref=far_out.at[split],
+            dst_ref=far_in.at[split],
+            send_sem=far_send.at[split],
+            recv_sem=far_recv.at[split],
+            device_id={"tp": opposite},
+            device_id_type=MESH,
+        )
+
+    def to_owner(split):
+        return pltpu.make_async_remote_copy(
+            src_ref=final.at[split],
+            dst_ref=out_ref.at[split],
+            send_sem=last_send.at[split],
+            recv_sem=last_recv.at[split],
             device_id={"ctx": to_ctx, "tp": to_tp},
             device_id_type=MESH,
         )
-        last.start()
-        last.wait()
-
-    @pl.when(stays)
-    def _():
-        keep = pltpu.make_async_copy(final, out_ref, local_sem)
-        keep.start()
-        keep.wait()
-
-    for index in range(4):
+
+    def keep(split):
+        return pltpu.make_async_copy(final.at[split], out_ref.at[split], local_sem.at[split])
+
+    window = 3
+    for piece in pieces[:window]:
+        launch(piece)
+    forward(pieces[0])
+    weight_copy(0).wait_recv()
+    weight_copy(1).wait_recv()
+    for number, piece in enumerate(pieces):
+        split, index = piece
+        if number + window < len(pieces):
+            launch(pieces[number + window])
+        if number + 1 < len(pieces):
+            forward(pieces[number + 1])
+        partial(piece)
+        if index < 2:
+            sending[split, index] = total[...].astype(bf16)
+            to_sibling(split, index).start()
+        elif index == 2:
+            to_sibling(split, 0).wait_recv()
+            far_out[split] = (total[...] + chip_in[split, 0].astype(f32)).astype(bf16)
+            to_opposite(split).start()
+        else:
+            to_sibling(split, 1).wait_recv()
+            to_opposite(split).wait_recv()
+            final[split] = (
+                total[...] + chip_in[split, 1].astype(f32) + far_in[split].astype(f32)
+            ).astype(bf16)
+
+            @pl.when(leaves)
+            def _():
+                to_owner(split).start()
+
+            @pl.when(stays)
+            def _():
+                keep(split).start()
+
+    for which in range(3):
         for step in range(1, groups):
-            copy_to(index, step).wait_send()
-    for index in range(2):
-        to_sibling(index).wait_send()
-    far.wait_send()
+            copy_to(which, step).wait_send()
+    for piece in pieces:
+        for slot in range(5):
+            piece_to(piece, slot).wait_send()
+        for slot in range(2):
+            pass_on(piece, direct[slot], slot).wait_send()
+    for which in range(2):
+        weight_copy(which).wait_send()
+    for split in range(splits):
+        for index in range(2):
+            to_sibling(split, index).wait_send()
+        to_opposite(split).wait_send()
+
+        @pl.when(leaves)
+        def _():
+            to_owner(split).wait()
+
+        @pl.when(stays)
+        def _():
+            keep(split).wait()
 
 
 def kernel_path(query_rows, key_rows, value_rows, filters, skip_gain, out_weight):
@@ -411,9 +451,12 @@
     groups = lax.axis_size("ctx")
     me = lax.axis_index("ctx")
     part = row_count // INNER
+    small = 16
+    splits = part // small
+    piece = small * INNER
     wide = INNER * LANES
     blocks = groups * part
-    half = out_weight.shape[1]
+    depth, half = out_weight.shape
     mixed_in = (key_rows.astype(f32) * value_rows.astype(f32)).astype(bf16)
 
     def by_group(rows):
@@ -424,59 +467,50 @@
     skip = jnp.tile(lax.dynamic_slice(skip_gain, (me * LANES,), (LANES,)), INNER)[None, :]
     forward, inverse, twist = block_tables(blocks)
     vmem = pl.BlockSpec(memory_space=pltpu.VMEM)
-    hbm = pl.BlockSpec(memory_space=pl.ANY)
     dma = pltpu.SemaphoreType.DMA
-    gated, other = pl.pallas_call(
-        functools.partial(convolve_kernel, groups),
-        out_shape=(
-            jax.ShapeDtypeStruct((blocks, wide), bf16),
-            jax.ShapeDtypeStruct(out_weight.shape, bf16),
-        ),
-        in_specs=[vmem, hbm, vmem, vmem, vmem, vmem],
-        out_specs=(vmem, hbm),
+    result = pl.pallas_call(
+        functools.partial(mixer_kernel, groups),
+        out_shape=jax.ShapeDtypeStruct((splits, piece, 2 * half), bf16),
+        in_specs=[vmem] * 6,
+        out_specs=pl.BlockSpec(memory_space=pl.ANY),
         scratch_shapes=[
             pltpu.VMEM((groups, part, wide), bf16),
             pltpu.VMEM((groups, part, wide), bf16),
             pltpu.VMEM((groups, part, wide), bf16),
             pltpu.VMEM((2 * blocks, wide), f32),
             pltpu.VMEM((2 * blocks, wide), f32),
+            pltpu.VMEM((blocks, wide), bf16),
+            pltpu.VMEM((depth, half), bf16),
+            pltpu.VMEM((splits, 4, groups, small, wide), bf16),
+            pltpu.VMEM((piece, chan_count), bf16),
+            pltpu.VMEM((piece, 2 * half), f32),
+            pltpu.VMEM((splits, 2, piece, 2 * half), bf16),
+            pltpu.VMEM((splits, 2, piece, 2 * half), bf16),
+            pltpu.VMEM((splits, piece, 2 * half), bf16),
+            pltpu.VMEM((splits, piece, 2 * half), bf16),
+            pltpu.VMEM((splits, piece, 2 * half), bf16),
             dma((3, groups)),
             dma((3, groups)),
             dma((2,)),
+            dma((2,)),
+            dma((splits, 4, 5)),
+            dma((splits, 4, groups)),
+            dma((splits, 4, 2)),
+            dma((splits, 2)),
+            dma((splits, 2)),
+            dma((splits,)),
+            dma((splits,)),
+            dma((splits,)),
+            dma((splits,)),
+            dma((splits,)),
         ],
         compiler_params=pltpu.CompilerParams(
             collective_id=0, has_side_effects=True, vmem_limit_bytes=40 * 2**20
         ),
-        name="convolve",
+        name="mixer",
     )(sent, out_weight, skip, jnp.asarray(forward), jnp.asarray(inverse), jnp.asarray(twist))
-    result = pl.pallas_call(
-        functools.partial(project_kernel, groups),
-        out_shape=jax.ShapeDtypeStruct((row_count, 2 * half), bf16),
-        in_specs=[vmem, vmem, vmem],
-        out_specs=hbm,
-        scratch_shapes=[
-            pltpu.VMEM((4, groups, part, wide), bf16),
-            pltpu.VMEM((row_count, chan_count), bf16),
-            pltpu.VMEM((row_count, 2 * half), f32),
-            pltpu.VMEM((2, row_count, 2 * half), bf16),
-            pltpu.VMEM((2, row_count, 2 * half), bf16),
-            pltpu.VMEM((row_count, 2 * half), bf16),
-            pltpu.VMEM((row_count, 2 * half), bf16),
-            pltpu.VMEM((row_count, 2 * half), bf16),
-            dma((4, groups)),
-            dma((4, groups)),
-            dma((2,)),
-            dma((2,)),
-            dma((2,)),
-            dma((2,)),
-            dma,
-        ],
-        compiler_params=pltpu.CompilerParams(
-            collective_id=1, has_side_effects=True, vmem_limit_bytes=40 * 2**20
-        ),
-        name="project",
-    )(gated, out_weight, other)
-    return result.reshape(INNER, part, 2 * half).transpose(1, 0, 2).reshape(row_count, 2 * half)
+    result = result.reshape(splits, INNER, small, 2 * half)
+    return result.transpose(0, 2, 1, 3).reshape(row_count, 2 * half)
 
 
 def on_device(query_rows, key_rows, value_rows, filters, skip_gain, out_weight):

time: 129 us -> 116 us (0.90)
  Pallas kernels: 123 us -> 106 us
  local copies, waits for them, and re-layouts: 4.9 us -> 8.32 us
  other arithmetic: 0.31 us -> 1.77 us
    pallas_call x2 -> x1, Pallas kernels: 123 us -> 106 us  [kernel_path(): pl.pallas_call(functools.partial(mixer_kernel, groups), out_shape=jax.Sha...]
    another operation x3, local copies, waits for them, and re-layouts: 0.67 us -> 3.04 us  [kernel_path(): jnp.stack([by_group(mixed_in), by_group(filters), by_group(query_rows)])]
    another operation x1, other arithmetic: 0.17 us -> 1.63 us  [kernel_path(): jnp.stack([by_group(mixed_in), by_group(filters), by_group(query_rows)])]
where the time goes in v1:
time: 116 us
  Pallas kernels  106 us (91%)
  local copies, waits for them, and re-layouts  8.32 us (7%)
  other arithmetic  1.77 us (2%)
    pallas_call x1, Pallas kernels, kernel_path(): pl.pallas_call(functools.partial(mixer_kernel, groups), out_shape=jax.Sha...  106 us
    unnamed x16, local copies, waits for them, and re-layouts  3.24 us
    another operation x3, local copies, waits for them, and re-layouts, kernel_path(): jnp.stack([by_group(mixed_in), by_group(filters), by_group(query_rows)])  3.04 us

profile of v1, /device:TPU:7, one launch (start us, length us, event | category | flops | bytes accessed | tf_op | source)
XLA Modules:
  0.0 115.8 jit_solution(17016729105074512458)
XLA Ops:
  0.0 0.0 copy-start
  0.0 0.0 copy-start.7
  0.0 1.0 copy-done
  1.0 0.1 copy_bitcast_fusion
  1.1 0.0 copy-start.5
  1.2 0.0 copy-start.6
  1.2 1.0 stack_reshape.11
  2.2 0.0 copy-done.7
  2.2 0.1 copy_bitcast_fusion.1
  2.3 1.0 stack_reshape.10
  3.3 0.0 copy-done.5
  3.3 0.0 copy-done.6
  3.3 0.1 copy_bitcast_fusion.2
  3.5 1.0 stack_reshape.9
  4.5 0.0 copy-start.1
  4.5 0.0 copy-start.4
  4.5 1.6 %pad_maximum_fusion.send_ref = bf16[3,8,32,1024]{3,2,1,0:T(8,128)(2,1)S(1)} fusion(bf16[1,8,32,1024]{3,2,1,0:T(8,128)(2,1)} %stack_reshape.11, bf16[1,8,32,1024]{3,2,1,0:T(8,128)(2,1)} %stack_reshape.10, bf16[1,8,32,1024]{3,2,1,0:T(8,128)(2,1)} %stack_reshape.9), kind=kLoop, calls=%fused_computation | loop fusion | flops 1572864 | bytes 3145728 | tf_op jit(solution)/shard_map/stack | solution.py:466
  6.1 0.8 dynamic_slice.3
  6.9 0.0 copy-done.1
  6.9 0.0 copy-done.4
  6.9 0.0 copy-start.2
  6.9 1.1 copy-done.2
  8.0 0.0 copy-start.3
  8.0 1.0 copy-done.3
  9.1 105.6 %mixer.1 = bf16[2,128,1024]{2,1,0:T(8,128)(2,1)S(1)} custom-call(bf16[3,8,32,1024]{3,2,1,0:T(8,128)(2,1)S(1)} %pad_maximum_fusion.send_ref, bf16[1024,512]{1,0:T(8,128)(2,1)S(1)} %copy-done.1, f32[1,1024]{1,0:T(1,128)S(1)} %bitcast.27, bf16[512,512]{1,0:T(8,128)(2,1)S(1)} %copy-done.3, bf16[256,1536]{1,0:T(8,128)(2,1)S(1)} %copy-done.2, ...), custom_call_target="tpu_custom_call" | custom-call | tf_op jit(solution)/shard_map/mixer/pallas_call | solution.py:471
  114.7 1.1 copy.13
  (1 shorter events, 0.0 us)
Async XLA Ops:
  0.0 1.0 copy-start
  0.0 2.2 %copy-start.7 = (bf16[256,1024]{1,0:T(8,128)(2,1)S(1)}, bf16[256,1024]{1,0:T(8,128)(2,1)}, u32[]{:S(2)}) copy-start(bf16[256,1024]{1,0:T(8,128)(2,1)} %param.12) | copy-start | bytes 1572868
  1.1 2.2 %copy-start.5 = (bf16[256,1024]{1,0:T(8,128)(2,1)S(1)}, bf16[256,1024]{1,0:T(8,128)(2,1)}, u32[]{:S(2)}) copy-start(bf16[256,1024]{1,0:T(8,128)(2,1)} %param.11) | copy-start | bytes 1572868
  1.2 2.1 %copy-start.6 = (bf16[256,1024]{1,0:T(8,128)(2,1)S(1)}, bf16[256,1024]{1,0:T(8,128)(2,1)}, u32[]{:S(2)}) copy-start(bf16[256,1024]{1,0:T(8,128)(2,1)} %param.10) | copy-start | bytes 1572868
  4.5 2.4 %copy-start.1 = (bf16[1024,512]{1,0:T(8,128)(2,1)S(1)}, bf16[1024,512]{1,0:T(8,128)(2,1)}, u32[]{:S(2)}) copy-start(bf16[1024,512]{1,0:T(8,128)(2,1)} %own_ref.1) | copy-start | bytes 3145732
  4.5 2.4 %copy-start.4 = (f32[2,256,128]{2,1,0:T(8,128)S(1)}, f32[2,256,128]{2,1,0:T(8,128)}, u32[]{:S(2)}) copy-start(f32[2,256,128]{2,1,0:T(8,128)} %constant.20.clone.twist_ref) | copy-start | bytes 786436
  6.9 1.1 copy-start.2
  8.0 1.0 copy-start.3

commit v2 on v1

--- a/solution.py
+++ b/solution.py
@@ -387,7 +387,7 @@
     def keep(split):
         return pltpu.make_async_copy(final.at[split], out_ref.at[split], local_sem.at[split])
 
-    window = 3
+    window = 2
     for piece in pieces[:window]:
         launch(piece)
     forward(pieces[0])

time: 116 us -> 113 us (0.974)
  Pallas kernels: 106 us -> 103 us
    pallas_call x1, Pallas kernels: 106 us -> 103 us  [kernel_path(): pl.pallas_call(functools.partial(mixer_kernel, groups), out_shape=jax.Sha...]
where the time goes in v2:
time: 113 us
  Pallas kernels  103 us (91%)
  local copies, waits for them, and re-layouts  8.32 us (7%)
  other arithmetic  1.77 us (2%)
    pallas_call x1, Pallas kernels, kernel_path(): pl.pallas_call(functools.partial(mixer_kernel, groups), out_shape=jax.Sha...  103 us
    unnamed x16, local copies, waits for them, and re-layouts  3.24 us
    another operation x3, local copies, waits for them, and re-layouts, kernel_path(): jnp.stack([by_group(mixed_in), by_group(filters), by_group(query_rows)])  3.04 us

profile of v2, /device:TPU:7, one launch (start us, length us, event | category | flops | bytes accessed | tf_op | source)
XLA Modules:
  0.0 112.7 jit_solution(1457577659695912679)
XLA Ops:
  0.0 0.0 copy-start
  0.0 0.0 copy-start.7
  0.0 1.0 copy-done
  1.0 0.1 copy_bitcast_fusion
  1.1 0.0 copy-start.5
  1.2 0.0 copy-start.6
  1.2 1.0 stack_reshape.11
  2.2 0.0 copy-done.7
  2.2 0.1 copy_bitcast_fusion.1
  2.3 1.0 stack_reshape.10
  3.3 0.0 copy-done.5
  3.3 0.0 copy-done.6
  3.3 0.1 copy_bitcast_fusion.2
  3.5 1.0 stack_reshape.9
  4.5 0.0 copy-start.1
  4.5 0.0 copy-start.4
  4.5 1.6 %pad_maximum_fusion.send_ref = bf16[3,8,32,1024]{3,2,1,0:T(8,128)(2,1)S(1)} fusion(bf16[1,8,32,1024]{3,2,1,0:T(8,128)(2,1)} %stack_reshape.11, bf16[1,8,32,1024]{3,2,1,0:T(8,128)(2,1)} %stack_reshape.10, bf16[1,8,32,1024]{3,2,1,0:T(8,128)(2,1)} %stack_reshape.9), kind=kLoop, calls=%fused_computation | loop fusion | flops 1572864 | bytes 3145728 | tf_op jit(solution)/shard_map/stack | solution.py:466
  6.1 0.8 dynamic_slice.3
  6.9 0.0 copy-done.1
  6.9 0.0 copy-done.4
  6.9 0.0 copy-start.2
  6.9 1.1 %copy-done.2 = bf16[256,1536]{1,0:T(8,128)(2,1)S(1)} copy-done((bf16[256,1536]{1,0:T(8,128)(2,1)S(1)}, bf16[256,1536]{1,0:T(8,128)(2,1)}, u32[]{:S(2)}) %copy-start.2) | copy-done | bytes 786456
  8.0 0.0 copy-start.3
  8.0 1.0 copy-done.3
  9.1 102.6 %mixer.1 = bf16[2,128,1024]{2,1,0:T(8,128)(2,1)S(1)} custom-call(bf16[3,8,32,1024]{3,2,1,0:T(8,128)(2,1)S(1)} %pad_maximum_fusion.send_ref, bf16[1024,512]{1,0:T(8,128)(2,1)S(1)} %copy-done.1, f32[1,1024]{1,0:T(1,128)S(1)} %bitcast.27, bf16[512,512]{1,0:T(8,128)(2,1)S(1)} %copy-done.3, bf16[256,1536]{1,0:T(8,128)(2,1)S(1)} %copy-done.2, ...), custom_call_target="tpu_custom_call" | custom-call | tf_op jit(solution)/shard_map/mixer/pallas_call | solution.py:471
  111.6 1.1 copy.13
  (1 shorter events, 0.0 us)
Async XLA Ops:
  0.0 1.0 copy-start
  0.0 2.2 %copy-start.7 = (bf16[256,1024]{1,0:T(8,128)(2,1)S(1)}, bf16[256,1024]{1,0:T(8,128)(2,1)}, u32[]{:S(2)}) copy-start(bf16[256,1024]{1,0:T(8,128)(2,1)} %param.12) | copy-start | bytes 1572868
  1.1 2.2 %copy-start.5 = (bf16[256,1024]{1,0:T(8,128)(2,1)S(1)}, bf16[256,1024]{1,0:T(8,128)(2,1)}, u32[]{:S(2)}) copy-start(bf16[256,1024]{1,0:T(8,128)(2,1)} %param.11) | copy-start | bytes 1572868
  1.2 2.1 %copy-start.6 = (bf16[256,1024]{1,0:T(8,128)(2,1)S(1)}, bf16[256,1024]{1,0:T(8,128)(2,1)}, u32[]{:S(2)}) copy-start(bf16[256,1024]{1,0:T(8,128)(2,1)} %param.10) | copy-start | bytes 1572868
  4.5 2.4 %copy-start.1 = (bf16[1024,512]{1,0:T(8,128)(2,1)S(1)}, bf16[1024,512]{1,0:T(8,128)(2,1)}, u32[]{:S(2)}) copy-start(bf16[1024,512]{1,0:T(8,128)(2,1)} %own_ref.1) | copy-start | bytes 3145732
  4.5 2.4 %copy-start.4 = (f32[2,256,128]{2,1,0:T(8,128)S(1)}, f32[2,256,128]{2,1,0:T(8,128)}, u32[]{:S(2)}) copy-start(f32[2,256,128]{2,1,0:T(8,128)} %constant.20.clone.twist_ref) | copy-start | bytes 786436
  6.9 1.1 %copy-start.2 = (bf16[256,1536]{1,0:T(8,128)(2,1)S(1)}, bf16[256,1536]{1,0:T(8,128)(2,1)}, u32[]{:S(2)}) copy-start(bf16[256,1536]{1,0:T(8,128)(2,1)} %constant.19.clone.inverse_ref) | copy-start | bytes 2359300
  8.0 1.0 copy-start.3
